TPU v7x, 32 devices: a whole 2x2x4 slice. The times are simulated.
32 devices in a mesh: store: 8 (over y, x, core), ctx: 4 (over z).
Axes of the slice: x: 2, y: 2, z: 4, core: 2. Of those that a mesh axis runs over, the one named last changes fastest.
Arguments:
- tokens: bfloat16 [1024, 8192], P('store'), may hold values from -6 to 6
- joined_weight: bfloat16 [8192, 8, 1280], P(None, 'ctx'), may hold values from -0.0625 to 0.0625
- down_weight: bfloat16 [64, 8192, 64], P('store', 'ctx'), may hold values from -0.0625 to 0.0625
- up_weight: bfloat16 [64, 64, 8, 1280], P('store', None, 'ctx'), may hold values from -0.75 to 0.75
- adapter_per_request: int32 [1024], replicated, may hold values from 0 to 63, as said below
- adapter_store_slot: int32 [64], replicated, may hold values from 0 to 63, as said below
- prefix_block_list: int32 [1024, 4], P('store'), may hold values from 0 to 63, as said below
- prefix_length: int32 [1024], P('store'), may hold values from 1 to 64, as said below
- key_value_pool: bfloat16 [1024, 8, 256], P(('store', 'ctx')), may hold values from -400 to 400
Outputs:
- attn: bfloat16 [1024, 8, 1024], P('store', 'ctx')
Inputs may be any that keep to these rules, and one draw needn't show every extreme that they name: `adapter_store_slot`: A permutation; slot s belongs to owner s // 8, which holds slots in store order. `adapter_per_request`: among the 128 requests of one store shard, at most 16 use adapters of one owner; on every shard one owner, the same for all shards, receives exactly 16. `prefix_block_list`: the 4 blocks of a request are distinct and lie in its store shard's range of 8 blocks, rows i * 128 to (i+1) * 128 - 1 using blocks i * 8 to (i+1) * 8 - 1. `prefix_length`: every store shard has a request of length 64.
All inputs are finite; a program needn't handle non-finite values.
Results may differ from a plain program's by a relative error of at most 0.02.
The roundings to bfloat16 on the way count: a program that leaves them out, or rounds other values in their place, can miss the bound.
Values may be sent and summed in bfloat16 or wider, within the bound.
A program may use at most 192 MiB of HBM per device.

v0:
```python
import jax
import jax.numpy as jnp
from jax import lax
from jax.sharding import PartitionSpec as P

QUERY_PER_KEY = 8
HEAD_SIZE = 128
CAP = 16
BLK = 16


ROPE_THETA = 500000.0
ADAPTER_SCALE = 2.0


def rotary_apply(vec, token_position):
    half = vec.shape[-1] // 2
    freq = jnp.power(ROPE_THETA, -(jnp.arange(half, dtype=jnp.float32) * 2.0 / vec.shape[-1]))
    angle = token_position[..., None] * freq
    cosine = jnp.cos(angle)
    sine = jnp.sin(angle)
    initial_part = vec[..., :half]
    second = vec[..., half:]
    return jnp.concatenate(
        [initial_part * cosine - second * sine, initial_part * sine + second * cosine], axis=-1
    )


def prefix_mask(local_ids, lens, group_blocks, blk):
    listed = local_ids.shape[1]
    equal = local_ids[:, :, None] == jnp.arange(group_blocks, dtype=jnp.int32)[None, None, :]
    start = jnp.sum(
        jnp.where(equal, (jnp.arange(listed, dtype=jnp.int32) * blk)[None, :, None], 0), axis=1
    )
    present = jnp.any(equal, axis=1)
    offset = jnp.arange(blk, dtype=jnp.int32)
    live = present[:, :, None] & (start[:, :, None] + offset[None, None, :] < lens[:, None, None])
    return live.reshape(local_ids.shape[0], group_blocks * blk)


def attend(query_rows, key_new, value_new, keys, value_rows, live):
    scale = 1.0 / HEAD_SIZE**0.5
    pool_scores = (
        jnp.einsum("rhgd,thd->rhgt", query_rows, keys, preferred_element_type=jnp.float32) * scale
    )
    own = (
        jnp.einsum("rhgd,rhd->rhg", query_rows, key_new, preferred_element_type=jnp.float32) * scale
    )
    mask = live[:, None, None, :]
    pool_scores = jnp.where(mask, pool_scores, -jnp.inf)
    top = jnp.maximum(jnp.max(pool_scores, axis=-1), own)
    prob = jnp.where(mask, jnp.exp(pool_scores - top[..., None]), 0.0)
    prob_own = jnp.exp(own - top)
    total = jnp.sum(prob, axis=-1) + prob_own
    prob_low = prob.astype(jnp.bfloat16)
    own_low = prob_own.astype(jnp.bfloat16)
    mixed = jnp.einsum("rhgt,thd->rhgd", prob_low, value_rows, preferred_element_type=jnp.float32)
    mixed = (
        mixed
        + own_low.astype(jnp.float32)[..., None] * value_new.astype(jnp.float32)[:, :, None, :]
    )
    mixed = mixed / total[..., None]
    return mixed.astype(jnp.bfloat16).reshape(query_rows.shape[0], query_rows.shape[1], -1)


def routing(adapter_per_request, adapter_store_slot, shards, request_shard, shard_adapters):
    adapters = adapter_store_slot.shape[0]
    match = adapter_per_request[:, None] == jnp.arange(adapters, dtype=jnp.int32)[None, :]
    store_slot = jnp.sum(jnp.where(match, adapter_store_slot[None, :], 0), axis=1).reshape(
        shards, request_shard
    )
    owner = store_slot // shard_adapters
    owner_hot = (owner[:, :, None] == jnp.arange(shards, dtype=jnp.int32)[None, None, :]).astype(
        jnp.int32
    )
    counted = jnp.cumsum(owner_hot, axis=1) - 1
    rank = jnp.sum(owner_hot * counted, axis=2)
    return (store_slot, owner, rank)


def body(
    tokens,
    joined_weight,
    down_weight,
    up_weight,
    adapter_per_request,
    adapter_store_slot,
    prefix_block_list,
    prefix_length,
    key_value_pool,
):
    n_store = lax.axis_size("store")
    n_ctx = lax.axis_size("ctx")
    shard = lax.axis_index("store")
    member = lax.axis_index("ctx")
    request_shard = tokens.shape[0]
    d_model = tokens.shape[1]
    shard_adapters = down_weight.shape[0]
    width_slice = down_weight.shape[1]
    head_slice = joined_weight.shape[1]
    column_list = joined_weight.shape[2]
    whole_group = lax.all_gather(key_value_pool, "ctx", axis=0, tiled=True)
    group = lax.dynamic_slice_in_dim(whole_group, member * head_slice, head_slice, 1)
    store_slot, owner, rank = routing(
        adapter_per_request, adapter_store_slot, n_store, request_shard, shard_adapters
    )
    owner_mine = lax.dynamic_index_in_dim(owner, shard, 0, keepdims=False)
    rank_mine = lax.dynamic_index_in_dim(rank, shard, 0, keepdims=False)
    dest = owner_mine * CAP + rank_mine
    x_local = lax.dynamic_slice_in_dim(tokens, member * width_slice, width_slice, 1)
    outgoing = jnp.zeros((n_store * CAP, width_slice), jnp.bfloat16).at[dest].set(x_local)
    received_parts = lax.all_to_all(
        outgoing.reshape(n_store, CAP, width_slice),
        "store",
        split_axis=0,
        concat_axis=0,
        tiled=True,
    )
    local_slot = store_slot % shard_adapters
    selected = (owner == shard)[:, :, None] & (
        rank[:, :, None] == jnp.arange(CAP, dtype=jnp.int32)[None, None, :]
    )
    adapter_hot = selected[:, :, :, None] & (
        local_slot[:, :, None, None]
        == jnp.arange(shard_adapters, dtype=jnp.int32)[None, None, None, :]
    )
    adapter_hot = jnp.any(adapter_hot, axis=1)
    value_partial = jnp.einsum(
        "hbm,gmq->hbgq", received_parts, down_weight, preferred_element_type=jnp.float32
    )
    shrunk_part = jnp.sum(jnp.where(adapter_hot[..., None], value_partial, 0.0), axis=2)
    shrunk = lax.psum(shrunk_part, "ctx").astype(jnp.bfloat16)
    spread_rows = jnp.where(
        adapter_hot[..., None], shrunk[:, :, None, :], jnp.zeros((), jnp.bfloat16)
    )
    adapter_update = jnp.einsum(
        "oxbl,blpj->oxpj", spread_rows, up_weight, preferred_element_type=jnp.float32
    ).astype(jnp.bfloat16)
    returned = lax.all_to_all(adapter_update, "store", split_axis=0, concat_axis=0, tiled=True)
    update_mine = returned.reshape(n_store * CAP, head_slice, column_list)[dest]
    plain_projection = jnp.dot(
        tokens,
        joined_weight.reshape(d_model, head_slice * column_list),
        preferred_element_type=jnp.float32,
    )
    joined_projection = plain_projection.reshape(
        request_shard, head_slice, column_list
    ) + ADAPTER_SCALE * update_mine.astype(jnp.float32)
    token_position = prefix_length.astype(jnp.float32)
    query_rows = rotary_apply(
        joined_projection[:, :, : QUERY_PER_KEY * HEAD_SIZE].reshape(
            request_shard, head_slice, QUERY_PER_KEY, HEAD_SIZE
        ),
        token_position[:, None, None],
    ).astype(jnp.bfloat16)
    key_new = rotary_apply(
        joined_projection[:, :, QUERY_PER_KEY * HEAD_SIZE : (QUERY_PER_KEY + 1) * HEAD_SIZE],
        token_position[:, None],
    ).astype(jnp.bfloat16)
    value_new = joined_projection[:, :, (QUERY_PER_KEY + 1) * HEAD_SIZE :].astype(jnp.bfloat16)
    group_blocks = key_value_pool.shape[0] * n_ctx // BLK
    live = prefix_mask(prefix_block_list - shard * group_blocks, prefix_length, group_blocks, BLK)
    return attend(
        query_rows, key_new, value_new, group[:, :, :HEAD_SIZE], group[:, :, HEAD_SIZE:], live
    )


def solution(mesh):
    in_specs = (
        P("store", None),
        P(None, "ctx", None),
        P("store", "ctx", None),
        P("store", None, "ctx", None),
        P(),
        P(),
        P("store", None),
        P("store"),
        P(("store", "ctx"), None, None),
    )
    out_specs = P("store", "ctx", None)
    return jax.shard_map(body, mesh=mesh, in_specs=in_specs, out_specs=out_specs, check_vma=False)
```

profile of v0, /device:TPU:0, one launch (start us, length us, event | category | flops | bytes accessed | tf_op | source)
XLA Modules:
  0.0 178.4 jit_solution(8919048933921384681)
XLA Ops:
  0.0 1.0 select_reduce_fusion.1
  1.0 0.1 copy.93
  1.1 2.5 %select_reduce_fusion = s32[8,128]{0,1:T(8,128)S(1)} fusion(s32[8,128]{0,1:T(8,128)S(1)} %copy.93), kind=kOutput, calls=%fused_computation.30 | output fusion | flops 1088512 | bytes 8192 | tf_op jit(solution)/shard_map/jit(cumsum)/reduce_window_sum | solution.py:76
  3.7 2.1 %scatter_custom_fusion = bf16[128,2048]{1,0:T(8,128)(2,1)} fusion(s32[128]{0:T(128)S(1)} %fusion.54, bf16[128,8192]{1,0:T(8,128)(2,1)S(1)} %copy-done, s32[]{:T(128)} %constant.35.clone.1, s32[]{:T(128)S(6)} %select_n.75, bf16[]{:T(256)} %constant.74.clone.1), kind=kCustom, calls=%fused_computation.28 | custom fusion | bytes 1048586 | tf_op jit(solution)/shard_map/scatter | solution.py:111
  5.8 5.2 %all-to-all-start = ((bf16[8,16,2048]{2,1,0:T(8,128)(2,1)}), bf16[8,16,2048]{2,1,0:T(8,128)(2,1)S(1)}, u32[]{:S(2)}, u32[]{:S(2)}) async-start(bf16[8,16,2048]{2,1,0:T(8,128)(2,1)} %bitcast.11), calls=%async_computation | async-start | bytes 1048576 | tf_op jit(solution)/shard_map/all_to_all | solution.py:112
  11.1 2.3 %and_reduce_fusion = pred[8,16,8]{2,1,0:T(8,128)(4,1)S(1)} fusion(pred[8,128,8]{1,2,0:T(8,128)(4,1)S(1)} %iota_compare_fusion.4, pred[8,128,16]{1,2,0:T(8,128)(4,1)S(1)} %fusion.42), kind=kLoop, calls=%fused_computation.36 | loop fusion | flops 261120 | bytes 25600 | tf_op jit(solution)/shard_map/reduce_or | solution.py:127
  13.6 7.2 %all-to-all-done = bf16[8,16,2048]{2,1,0:T(8,128)(2,1)S(1)} async-done(((bf16[8,16,2048]{2,1,0:T(8,128)(2,1)}), bf16[8,16,2048]{2,1,0:T(8,128)(2,1)S(1)}, u32[]{:S(2)}, u32[]{:S(2)}) %all-to-all-start) | async-done | bytes 524320 | tf_op jit(solution)/shard_map/all_to_all | solution.py:112
  20.8 2.8 %fusion.16 = f32[8,16,64]{2,1,0:T(8,128)S(1)} fusion(bf16[8,2048,64]{1,2,0:T(8,128)(2,1)} %param.11, bf16[8,16,2048]{2,1,0:T(8,128)(2,1)S(1)} %all-to-all-done, pred[8,16,8]{1,2,0:T(8,128)(4,1)S(1)} %copy.95), kind=kOutput, calls=%fused_computation.18 | convolution fusion | flops 268558336 | bytes 2655232 | tf_op jit(solution)/shard_map/hbm,gmq->hbgq/dot_general | solution.py:128
  23.5 19.9 %psum.7 = bf16[8,16,64]{2,1,0:T(8,128)(2,1)S(1)} all-reduce(f32[8,16,64]{2,1,0:T(8,128)S(1)} %fusion.16), channel_id=1, replica_groups=mesh['store'=8,'ctx'=4] {'ctx'}, use_global_device_ids=true, to_apply=%region_8.9 | all-reduce | flops 8192 | bytes 49152 | tf_op jit(solution)/shard_map/psum | solution.py:132
  43.4 3.3 %fusion.2 = bf16[8,16,2,1280]{3,1,2,0:T(8,128)(2,1)} fusion(bf16[8,64,2,1280]{3,2,1,0:T(2,128)(2,1)} %param.12, pred[8,16,8]{1,2,0:T(8,128)(4,1)S(1)} %copy.95, bf16[8,16,64]{2,1,0:T(8,128)(2,1)S(1)} %psum.7), kind=kOutput, calls=%fused_computation.5 | convolution fusion | flops 335937536 | bytes 3294208 | tf_op jit(solution)/shard_map/oxbl,blpj->oxpj/dot_general | solution.py:136
  46.7 3.5 %all-to-all-start.1 = ((bf16[8,16,2,1280]{3,1,2,0:T(8,128)(2,1)}), bf16[8,16,2,1280]{3,1,2,0:T(8,128)(2,1)S(1)}, u32[]{:S(2)}, u32[]{:S(2)}) async-start(bf16[8,16,2,1280]{3,1,2,0:T(8,128)(2,1)} %fusion.2), calls=%async_computation.1 | async-start | bytes 1310720 | tf_op jit(solution)/shard_map/all_to_all | solution.py:139
  50.3 28.0 %copy.120 = bf16[1024,8,2,1280]{3,1,2,0:T(8,128)(2,1)} copy(bf16[1024,8,2,1280]{3,2,1,0:T(2,128)(2,1)} %bitcast.128) | data formatting | bytes 83886080
  78.3 50.3 %copy.92 = bf16[2560,8192]{1,0:T(8,128)(2,1)} copy(bf16[2560,8192]{0,1:T(8,128)(2,1)} %bitcast.127) | data formatting | bytes 83886080 | tf_op jit(solution)/shard_map/dot_general | solution.py:141
  128.8 17.0 %all_gather.3 = bf16[128,8,256]{2,0,1:T(8,128)(2,1)} all-gather(bf16[32,8,256]{2,0,1:T(8,128)(2,1)S(1)} %copy.91), channel_id=1, replica_groups=mesh['store'=8,'ctx'=4] {'ctx'}, dimensions={0}, use_global_device_ids=true | all-gather | bytes 655360 | tf_op jit(solution)/shard_map/all_gather | solution.py:102
  145.8 0.3 multiply_cosine_fusion
  146.2 0.7 copy.99
  146.9 2.7 %gather_fusion = bf16[128,2,1280]{2,1,0:T(2,128)(2,1)} fusion(bf16[128,2,1280]{2,1,0:T(2,128)(2,1)S(1)} %copy.99, s32[1024]{0:T(1024)S(1)} %pad_clamp_fusion), kind=kCustom, calls=%fused_computation | custom fusion | bytes 1311232 | tf_op jit(solution)/shard_map/gather | solution.py:140
  149.6 19.5 %convolution_add_fusion = f32[128,2,1280]{2,0,1:T(8,128)S(1)} fusion(bf16[2,1280,8192]{2,1,0:T(8,128)(2,1)} %bitcast.126, bf16[128,8192]{1,0:T(8,128)(2,1)S(1)} %copy-done, bf16[128,2,1280]{2,1,0:T(2,128)(2,1)} %gather_fusion), kind=kOutput, calls=%fused_computation.6 | convolution fusion | flops 5369692160 | bytes 46006272 | tf_op jit(solution)/shard_map/dot_general | solution.py:141
  169.2 0.1 slice.38
  169.3 0.7 fusion.40
  169.9 0.2 copy.121
  170.1 0.3 fusion.57
  170.5 0.1 subtract_convert_fusion.1
  170.6 0.4 subtract_convert_fusion
  171.0 0.3 pad_maximum_fusion
  171.4 0.7 copy-done.1
  172.1 0.5 fusion.29
  172.7 1.4 fusion.58
  174.1 0.2 fusion.19
  174.3 0.1 copy.105
  174.4 2.0 %fusion.12 = bf16[128,2,8,128]{0,3,2,1:T(8,128)(2,1)} fusion(f32[128,2,8,128]{0,3,2,1:T(8,128)S(1)} %get-tuple-element.18, f32[128,2,8]{0,2,1:T(8,128)S(1)} %get-tuple-element.12, f32[128,2,128]{0,2,1:T(8,128)S(1)} %copy.105, f32[128,2,8]{0,2,1:T(8,128)S(1)} %get-tuple-element.11, f32[128,2,8]{0,2,1:T(8,128)S(1)} %fusion.45, ...), kind=kOutput, calls=%fused_computation.16 | convolution fusion | flops 68943872 | bytes 1810440 | tf_op jit(solution)/shard_map/rhgt,thd->rhgd/dot_general | solution.py:57
  176.4 2.0 %copy.106 = bf16[128,2,1024]{2,1,0:T(2,128)(2,1)} copy(bf16[128,2,1024]{0,2,1:T(8,128)(2,1)} %bitcast.132) | data formatting | bytes 1048576 | tf_op jit(solution)/shard_map/reshape | solution.py:63
  (35 shorter events, 0.8 us)
Async XLA Ops:
  0.0 3.7 %copy-start = (bf16[128,8192]{1,0:T(8,128)(2,1)S(1)}, bf16[128,8192]{1,0:T(8,128)(2,1)}, u32[]{:S(2)}) copy-start(bf16[128,8192]{1,0:T(8,128)(2,1)} %param.9) | copy-start | bytes 6291460
  0.0 13.4 %copy-start.4 = (s32[128,4]{0,1:T(4,128)S(1)}, s32[128,4]{0,1:T(4,128)}, u32[]{:S(2)}) copy-start(s32[128,4]{0,1:T(4,128)} %param.15) | copy-start | bytes 6148
  5.8 14.9 %all-to-all-start = ((bf16[8,16,2048]{2,1,0:T(8,128)(2,1)}), bf16[8,16,2048]{2,1,0:T(8,128)(2,1)S(1)}, u32[]{:S(2)}, u32[]{:S(2)}) async-start(bf16[8,16,2048]{2,1,0:T(8,128)(2,1)} %bitcast.11), calls=%async_computation | async-start | bytes 1048576 | tf_op jit(solution)/shard_map/all_to_all | solution.py:112
  46.7 99.4 %all-to-all-start.1 = ((bf16[8,16,2,1280]{3,1,2,0:T(8,128)(2,1)}), bf16[8,16,2,1280]{3,1,2,0:T(8,128)(2,1)S(1)}, u32[]{:S(2)}, u32[]{:S(2)}) async-start(bf16[8,16,2,1280]{3,1,2,0:T(8,128)(2,1)} %fusion.2), calls=%async_computation.1 | async-start | bytes 1310720 | tf_op jit(solution)/shard_map/all_to_all | solution.py:139
  78.3 50.3 %copy-start.5 = (s32[128]{0:T(128)S(1)}, s32[128]{0:T(128)}, u32[]{:S(2)}) copy-start(s32[128]{0:T(128)} %param.16) | copy-start | bytes 1540
  78.3 50.3 %copy-start.3 = (bf16[32,8,256]{2,1,0:T(8,128)(2,1)S(1)}, bf16[32,8,256]{2,1,0:T(8,128)(2,1)}, u32[]{:S(2)}) copy-start(bf16[32,8,256]{2,1,0:T(8,128)(2,1)} %param.17) | copy-start | bytes 393220
  171.3 0.8 copy-start.1
  172.1 2.2 %copy-start.2 = (f32[128,2,128]{2,0,1:T(8,128)S(1)}, f32[128,2,128]{2,0,1:T(8,128)}, u32[]{:S(2)}) copy-start(f32[128,2,128]{2,0,1:T(8,128)} %fusion.40) | copy-start | bytes 393220
where the time goes:
time: 180 us; the launch traced here: 178 us
  local copies, waits for them, and re-layouts  87.8 us (49%)
  blocking collectives  36.9 us (20%)
  matrix products  29.4 us (16%)
  starting transfers between devices  8.71 us (5%)
  other arithmetic  8.1 us (4%)
  waiting for transfers between devices  7.2 us (4%)
    dot_general x1, local copies, waits for them, and re-layouts, body(): jnp.dot(tokens, joined_weight.reshape(d_model, head_slice * column_list),...  50.3 us
    unnamed x15, local copies, waits for them, and re-layouts  29 us
    psum x1, blocking collectives, body(): shrunk = lax.psum(shrunk_part, 'ctx').astype(jnp.bfloat16)  19.9 us
    dot_general x1, matrix products, body(): jnp.dot(tokens, joined_weight.reshape(d_model, head_slice * column_list),...  19.5 us
    all_gather x1, blocking collectives, body(): whole_group = lax.all_gather(key_value_pool, 'ctx', axis=0, tiled=True)  17 us
    all_to_all x1, waiting for transfers between devices, body(): lax.all_to_all(outgoing.reshape(n_store, CAP, width_slice), 'store', spli...  7.2 us
    all_to_all x1, starting transfers between devices, body(): lax.all_to_all(outgoing.reshape(n_store, CAP, width_slice), 'store', spli...  5.17 us
  transfers between devices with their start and end apart: 2, of which 1 were waited for; matrix products, arithmetic and copies ran while one was open for 46% of the time, Pallas kernels for 0%

commit v1 on v0

v1 whole, which is shorter than its diff:
```python
import functools

import jax
import jax.numpy as jnp
from jax import lax
from jax.experimental import pallas as pl
from jax.experimental.pallas import tpu as pltpu
from jax.sharding import PartitionSpec as P

QUERY_PER_KEY = 8
HEAD_SIZE = 128
CAP = 16
BLK = 16
LANES = 128
DEPTH = 512
PARTS = (6, 4, 6)

ROPE_THETA = 500000.0
ADAPTER_SCALE = 2.0


def spread_columns(tok_ref, e_ref, z_ref):
    rows = tok_ref.shape[0]
    for c in range(tok_ref.shape[1] // LANES):
        wide = jnp.dot(
            tok_ref[:, c * LANES : (c + 1) * LANES], e_ref[...], preferred_element_type=jnp.float32
        ).astype(jnp.bfloat16)
        cols = slice(c * 2 * LANES, (c + 1) * 2 * LANES)
        z_ref[:rows, cols] = wide[:, : 2 * LANES]
        z_ref[rows:, cols] = wide[:, 2 * LANES :]


def projection_kernel(columns, has_base, *refs):
    tiles = columns // LANES
    tok_ref = refs[0]
    w_refs = refs[1 : 1 + tiles]
    base_ref = refs[1 + tiles] if has_base else None
    out_ref, e_ref, z_ref = refs[-3:]
    depth = tok_ref.shape[1]

    @pl.when(pl.program_id(0) == 0)
    def _():
        row = lax.broadcasted_iota(jnp.int32, (LANES, 4 * LANES), 0)
        col = lax.broadcasted_iota(jnp.int32, (LANES, 4 * LANES), 1)
        goal = jnp.where(col < 2 * LANES, 2 * row, 2 * row + 1 + 2 * LANES)
        e_ref[...] = (col == goal).astype(jnp.float32).astype(jnp.bfloat16)
        if has_base:
            out_ref[...] = base_ref[...]
        else:
            out_ref[...] = jnp.zeros_like(out_ref)

    spread_columns(tok_ref, e_ref, z_ref)
    for j in range(0, tiles, 2):
        pair = [w_refs[i].reshape(2 * depth, LANES)[...] for i in range(j, min(j + 2, tiles))]
        weight = jnp.concatenate(pair, axis=1) if len(pair) > 1 else pair[0]
        cols = slice(j * LANES, j * LANES + weight.shape[1])
        out_ref[:, cols] += jnp.dot(z_ref[...], weight, preferred_element_type=jnp.float32)


def projection_part(tokens, joined_weight, base, first, steps):
    rows = tokens.shape[0]
    columns = joined_weight.shape[2]
    tiles = columns // LANES
    in_specs = [pl.BlockSpec((rows, DEPTH), lambda k: (0, k + first))]
    for c in range(tiles):
        in_specs.append(
            pl.BlockSpec((DEPTH, 2, LANES), functools.partial(lambda c, k: (k + first, 0, c), c))
        )
    operands = [tokens] + [joined_weight] * tiles
    if base is not None:
        in_specs.append(pl.BlockSpec((2 * rows, columns), lambda k: (0, 0)))
        operands.append(base)
    return pl.pallas_call(
        functools.partial(projection_kernel, columns, base is not None),
        grid=(steps,),
        in_specs=in_specs,
        out_specs=pl.BlockSpec((2 * rows, columns), lambda k: (0, 0)),
        out_shape=jax.ShapeDtypeStruct((2 * rows, columns), jnp.float32),
        scratch_shapes=[
            pltpu.VMEM((LANES, 4 * LANES), jnp.bfloat16),
            pltpu.VMEM((2 * rows, 2 * DEPTH), jnp.bfloat16),
        ],
        compiler_params=pltpu.CompilerParams(vmem_limit_bytes=32 << 20),
        cost_estimate=pl.CostEstimate(
            flops=8 * rows * DEPTH * steps * columns,
            bytes_accessed=4 * DEPTH * steps * columns,
            transcendentals=0,
        ),
        name="projection",
    )(*operands)


def plain_projection(tokens, joined_weight):
    rows, width = tokens.shape
    heads, columns = joined_weight.shape[1:]
    if heads == 2:
        total = width // DEPTH
        parts = PARTS if sum(PARTS) == total else (total,)
        first, base = 0, None
        for steps in parts:
            base = projection_part(tokens, joined_weight, base, first, steps)
            first += steps
        return base
    out = jnp.dot(
        tokens, joined_weight.reshape(width, heads * columns), preferred_element_type=jnp.float32
    )
    return jnp.transpose(out.reshape(rows, heads, columns), (1, 0, 2)).reshape(heads * rows, columns)


def attention_kernel(plain_ref, back_ref, dest_ref, len_ref, ids_ref, cos_ref, sin_ref, pool_ref, out_ref):
    heads, rows, _ = out_ref.shape
    slots = back_ref.shape[0] * back_ref.shape[2]
    count = pool_ref.shape[0] * pool_ref.shape[2]
    scale = 1.0 / HEAD_SIZE**0.5
    pick = (lax.broadcasted_iota(jnp.int32, (rows, slots), 1) == dest_ref[...]).astype(
        jnp.float32
    ).astype(jnp.bfloat16)
    token = lax.broadcasted_iota(jnp.int32, (rows, count), 1)
    block, offset = token // BLK, token % BLK
    lens = len_ref[...]
    live = jnp.zeros((rows, count), jnp.float32)
    for j in range(ids_ref.shape[1]):
        hit = (ids_ref[:, j : j + 1] == block) & (offset + j * BLK < lens)
        live = jnp.where(hit, 1.0, live)
    cosine, sine = cos_ref[...], sin_ref[...]

    def rope(v):
        return (v * cosine + pltpu.roll(v, HEAD_SIZE // 2, 1) * sine).astype(jnp.bfloat16)

    for h in range(heads):
        update = jnp.dot(
            pick, back_ref[:, h].reshape(slots, back_ref.shape[3]), preferred_element_type=jnp.float32
        )
        joined = plain_ref[h * rows : (h + 1) * rows, :] + ADAPTER_SCALE * update
        key_new = rope(joined[:, QUERY_PER_KEY * HEAD_SIZE : (QUERY_PER_KEY + 1) * HEAD_SIZE])
        key_new = key_new.astype(jnp.float32)
        value_new = joined[:, (QUERY_PER_KEY + 1) * HEAD_SIZE :].astype(jnp.bfloat16)
        value_new = value_new.astype(jnp.float32)
        keys = pool_ref[:, h, :, :HEAD_SIZE].reshape(count, HEAD_SIZE)
        value_rows = pool_ref[:, h, :, HEAD_SIZE:].reshape(count, HEAD_SIZE)
        for g in range(QUERY_PER_KEY):
            query = rope(joined[:, g * HEAD_SIZE : (g + 1) * HEAD_SIZE])
            scores = (
                lax.dot_general(
                    query, keys, (((1,), (1,)), ((), ())), preferred_element_type=jnp.float32
                )
                * scale
            )
            own = jnp.sum(query.astype(jnp.float32) * key_new, axis=1, keepdims=True) * scale
            scores = jnp.where(live > 0.0, scores, -jnp.inf)
            top = jnp.maximum(jnp.max(scores, axis=1, keepdims=True), own)
            prob = jnp.exp(scores - top)
            prob_own = jnp.exp(own - top)
            total = jnp.sum(prob, axis=1, keepdims=True) + prob_own
            mixed = jnp.dot(prob.astype(jnp.bfloat16), value_rows, preferred_element_type=jnp.float32)
            mixed = mixed + prob_own.astype(jnp.bfloat16).astype(jnp.float32) * value_new
            out_ref[h, :, g * HEAD_SIZE : (g + 1) * HEAD_SIZE] = (mixed / total).astype(jnp.bfloat16)


def attention(plain, back, dest, lens, ids, cosine, sine, pool, rows, heads):
    return pl.pallas_call(
        attention_kernel,
        out_shape=jax.ShapeDtypeStruct((heads, rows, QUERY_PER_KEY * HEAD_SIZE), jnp.bfloat16),
        in_specs=[pl.BlockSpec(memory_space=pltpu.VMEM)] * 8,
        out_specs=pl.BlockSpec(memory_space=pltpu.VMEM),
        compiler_params=pltpu.CompilerParams(vmem_limit_bytes=24 << 20),
        name="attention",
    )(plain, back, dest, lens, ids, cosine, sine, pool)


def routing(adapter_per_request, adapter_store_slot, shards, request_shard, shard_adapters, shard):
    adapters = adapter_store_slot.shape[0]
    match = adapter_per_request[:, None] == jnp.arange(adapters, dtype=jnp.int32)[None, :]
    store_slot = jnp.sum(jnp.where(match, adapter_store_slot[None, :], 0), axis=1).reshape(
        shards, request_shard
    )
    owner = store_slot // shard_adapters
    local = store_slot - owner * shard_adapters
    index = jnp.arange(request_shard, dtype=jnp.int32)
    earlier = index[:, None] < index[None, :]
    same = owner[:, :, None] == owner[:, None, :]
    rank = jnp.sum((same & earlier[None]).astype(jnp.int32), axis=1)
    owner_mine = lax.dynamic_index_in_dim(owner, shard, 0, keepdims=False)
    rank_mine = lax.dynamic_index_in_dim(rank, shard, 0, keepdims=False)
    dest = owner_mine * CAP + rank_mine
    place = jnp.where(owner == shard, rank, -1)
    chosen = place[:, None, :] == jnp.arange(CAP, dtype=jnp.int32)[None, :, None]
    arrived = jnp.sum(jnp.where(chosen, local[:, None, :] + 1, 0), axis=2) - 1
    return dest, arrived


def body(
    tokens,
    joined_weight,
    down_weight,
    up_weight,
    adapter_per_request,
    adapter_store_slot,
    prefix_block_list,
    prefix_length,
    key_value_pool,
):
    n_store = lax.axis_size("store")
    n_ctx = lax.axis_size("ctx")
    shard = lax.axis_index("store")
    member = lax.axis_index("ctx")
    request_shard = tokens.shape[0]
    shard_adapters, width_slice, rank_size = down_weight.shape
    head_slice = joined_weight.shape[1]
    columns = joined_weight.shape[2]
    pool_rows = key_value_pool.shape[0]

    dest, arrived = routing(
        adapter_per_request, adapter_store_slot, n_store, request_shard, shard_adapters, shard
    )
    slots = n_store * CAP
    x_local = lax.dynamic_slice_in_dim(tokens, member * width_slice, width_slice, 1)
    place = (jnp.arange(slots, dtype=jnp.int32)[:, None] == dest[None, :]).astype(jnp.bfloat16)
    outgoing = jnp.dot(place, x_local, preferred_element_type=jnp.float32).astype(jnp.bfloat16)
    received = lax.all_to_all(
        outgoing.reshape(n_store, CAP, width_slice), "store", split_axis=0, concat_axis=0, tiled=True
    )
    pool = jnp.transpose(key_value_pool, (1, 0, 2)).reshape(
        n_ctx, head_slice, pool_rows, 2 * HEAD_SIZE
    )
    pool = lax.all_to_all(pool, "ctx", split_axis=0, concat_axis=0, tiled=True)

    hot = arrived[:, :, None] == jnp.arange(shard_adapters, dtype=jnp.int32)[None, None, :]
    value_partial = jnp.einsum(
        "hbm,gmq->hbgq", received, down_weight, preferred_element_type=jnp.float32
    )
    shrunk_part = jnp.sum(jnp.where(hot[..., None], value_partial, 0.0), axis=2)
    copies = jnp.broadcast_to(shrunk_part[None], (n_ctx,) + shrunk_part.shape)
    partials = lax.all_to_all(copies, "ctx", split_axis=0, concat_axis=0, tiled=True)
    shrunk = jnp.sum(partials, axis=0).astype(jnp.bfloat16)
    spread_rows = jnp.where(hot[..., None], shrunk[:, :, None, :], jnp.zeros((), jnp.bfloat16))
    update = jnp.einsum(
        "oxbl,blpj->opxj", spread_rows, up_weight, preferred_element_type=jnp.float32
    ).astype(jnp.bfloat16)
    back = lax.all_to_all(update, "store", split_axis=0, concat_axis=0, tiled=True)

    plain = plain_projection(tokens, joined_weight)

    half = HEAD_SIZE // 2
    freq = jnp.power(ROPE_THETA, -(jnp.arange(half, dtype=jnp.float32) * 2.0 / HEAD_SIZE))
    angle = prefix_length.astype(jnp.float32)[:, None] * freq
    cosine, sine = jnp.cos(angle), jnp.sin(angle)
    group_blocks = pool_rows * n_ctx // BLK
    out = attention(
        plain,
        back,
        dest[:, None],
        prefix_length[:, None],
        prefix_block_list - shard * group_blocks,
        jnp.concatenate([cosine, cosine], axis=1),
        jnp.concatenate([-sine, sine], axis=1),
        pool,
        request_shard,
        head_slice,
    )
    return jnp.transpose(out, (1, 0, 2))


def solution(mesh):
    in_specs = (
        P("store", None),
        P(None, "ctx", None),
        P("store", "ctx", None),
        P("store", None, "ctx", None),
        P(),
        P(),
        P("store", None),
        P("store"),
        P(("store", "ctx"), None, None),
    )
    out_specs = P("store", "ctx", None)
    return jax.shard_map(body, mesh=mesh, in_specs=in_specs, out_specs=out_specs, check_vma=False)
```

time: 180 us -> 93.4 us (0.52)
  local copies, waits for them, and re-layouts: 87.8 us -> 21.9 us
  blocking collectives: 36.9 us -> 0 us
  Pallas kernels: 0 us -> 35.6 us
  matrix products: 29.4 us -> 6.63 us
  starting transfers between devices: 8.71 us -> 19.5 us
  waiting for transfers between devices: 7.2 us -> 0.01 us
    dot_general x2 -> x0, local copies, waits for them, and re-layouts: 50.3 us -> none  [the longest x1 50.3 us: body(): jnp.dot(tokens, joined_weight.reshape(d_model, head_slice * column_list),...]
    pallas_call x0 -> x4, Pallas kernels: none -> 35.6 us  [the longest x3 30.9 us: projection_part(): pl.pallas_call(functools.partial(projection_kernel, columns, base is not...]
    dot_general x6 -> x3, matrix products: 29.4 us -> 6.63 us  [the longest x1 3.28 us: body(): jnp.einsum('oxbl,blpj->opxj', spread_rows, up_weight, preferred_element_t...]
    psum x1 -> x0, blocking collectives: 19.9 us -> none  [body(): shrunk = lax.psum(shrunk_part, 'ctx').astype(jnp.bfloat16)]
    all_gather x1 -> x0, blocking collectives: 17 us -> none  [body(): whole_group = lax.all_gather(key_value_pool, 'ctx', axis=0, tiled=True)]
    unnamed x15 -> x37, local copies, waits for them, and re-layouts: 29 us -> 17.8 us
    all_to_all x1 -> x3, starting transfers between devices: 3.54 us -> 14.3 us  [the longest x1 5.07 us: body(): pool = lax.all_to_all(pool, 'ctx', split_axis=0, concat_axis=0, tiled=True)]
    all_to_all x1, waiting for transfers between devices: 7.2 us -> 0.01 us  [body(): lax.all_to_all(outgoing.reshape(n_store, CAP, width_slice), 'store', spli...]
  transfers between devices with their start and end apart: 2 -> 4, of which waited for: 1 -> 0; matrix products, arithmetic and copies ran while one was open for 46% -> 17% of each run, Pallas kernels for 0% -> 34%
where the time goes in v1:
time: 93.4 us; the launch traced here: 92 us
  Pallas kernels  35.6 us (38%)
  local copies, waits for them, and re-layouts  21.9 us (23%)
  starting transfers between devices  19.5 us (21%)
  other arithmetic  8.15 us (9%)
  matrix products  6.63 us (7%)
    pallas_call x3, Pallas kernels, projection_part(): pl.pallas_call(functools.partial(projection_kernel, columns, base is not...  30.9 us
    unnamed x37, local copies, waits for them, and re-layouts  17.8 us
    all_to_all x1, starting transfers between devices, body(): lax.all_to_all(outgoing.reshape(n_store, CAP, width_slice), 'store', spli...  5.18 us
    all_to_all x1, starting transfers between devices, body(): pool = lax.all_to_all(pool, 'ctx', split_axis=0, concat_axis=0, tiled=True)  5.07 us
    all_to_all x1, starting transfers between devices, body(): lax.all_to_all(copies, 'ctx', split_axis=0, concat_axis=0, tiled=True)  4.87 us
    pallas_call x1, Pallas kernels, attention(): pl.pallas_call(attention_kernel, out_shape=jax.ShapeDtypeStruct((heads, r...  4.76 us
    all_to_all x1, starting transfers between devices, body(): lax.all_to_all(update, 'store', split_axis=0, concat_axis=0, tiled=True)  4.39 us
    dot_general x1, matrix products, body(): jnp.einsum('oxbl,blpj->opxj', spread_rows, up_weight, preferred_element_t...  3.28 us
  transfers between devices with their start and end apart: 4, of which 0 were waited for; matrix products, arithmetic and copies ran while one was open for 17% of the time, Pallas kernels for 34%

profile of v1, /device:TPU:0, one launch (start us, length us, event | category | flops | bytes accessed | tf_op | source)
XLA Modules:
  0.0 92.0 jit_solution(17887813836953662282)
XLA Ops:
  0.0 1.0 %select_reduce_fusion = s32[1024]{0:T(1024)S(1)} fusion(s32[64]{0:T(128)} %param.14, s32[1024]{0:T(1024)} %param.13), kind=kLoop, calls=%fused_computation.15 | loop fusion | flops 195584 | bytes 8448 | tf_op jit(solution)/shard_map/reduce_sum | solution.py:174
  1.3 2.1 %convolution_convert_fusion = bf16[128,2048]{1,0:T(8,128)(2,1)} fusion(bf16[128,8192]{1,0:T(8,128)(2,1)} %refs_0_.5, s32[]{:T(128)S(6)} %select_n.56, s32[128]{0:T(128)S(1)} %bitcast.66), kind=kOutput, calls=%fused_computation.5 | convolution fusion | flops 67387392 | bytes 1049092 | tf_op jit(solution)/shard_map/dot_general | solution.py:219
  3.4 5.2 %all-to-all-start = ((bf16[8,16,2048]{2,1,0:T(8,128)(2,1)}), bf16[8,16,2048]{2,1,0:T(8,128)(2,1)S(1)}, u32[]{:S(2)}, u32[]{:S(2)}) async-start(bf16[8,16,2048]{2,1,0:T(8,128)(2,1)} %bitcast.2), calls=%async_computation | async-start | bytes 1048576 | tf_op jit(solution)/shard_map/all_to_all | solution.py:220
  8.8 0.7 copy.26.dest_ref
  12.0 0.8 pad_maximum_fusion
  12.8 1.6 %copy-done.1 = bf16[128,8192]{1,0:T(8,128)(2,1)S(1)} copy-done((bf16[128,8192]{1,0:T(8,128)(2,1)S(1)}, bf16[128,8192]{1,0:T(8,128)(2,1)}, u32[]{:S(2)}) %copy-start.1) | copy-done | bytes 2097176
  14.4 11.3 %projection.3.refs_11_ = f32[256,1280]{1,0:T(8,128)S(1)} custom-call(bf16[128,8192]{1,0:T(8,128)(2,1)S(1)} %copy-done.1, bf16[8192,2,1280]{2,1,0:T(2,128)(2,1)} %refs_10_.5, bf16[8192,2,1280]{2,1,0:T(2,128)(2,1)} %refs_10_.5, bf16[8192,2,1280]{2,1,0:T(2,128)(2,1)} %refs_10_.5, bf16[8192,2,1280]{2,1,0:T(2,128)(2,1)} %refs_10_.5, ...), custom_call_target="tpu_custom_call" | custom-call | flops 4026531840 | bytes 15728640 | tf_op jit(solution)/shard_map/projection/pallas_call | solution.py:73
  25.8 1.1 %copy-done.6 = f32[256,1280]{1,0:T(8,128)} copy-done((f32[256,1280]{1,0:T(8,128)}, f32[256,1280]{1,0:T(8,128)S(1)}, u32[]{:S(2)}) %copy-start.6) | copy-done | bytes 1310744
  26.9 1.2 %fusion.13 = f32[8,16,64]{2,1,0:T(8,128)S(1)} fusion(bf16[8,2048,64]{1,2,0:T(8,128)(2,1)S(1)} %copy-done, bf16[8,16,2048]{2,1,0:T(8,128)(2,1)S(1)} %all-to-all-done, pred[8,16,8]{1,2,0:T(8,128)(4,1)S(1)} %iota_compare_fusion.5), kind=kOutput, calls=%fused_computation.9 | convolution fusion | flops 268558336 | bytes 2655232 | tf_op jit(solution)/shard_map/hbm,gmq->hbgq/dot_general | solution.py:229
  28.1 0.8 reshape.156
  28.9 4.9 %all-to-all-start.1 = ((f32[4,1,8192]{2,1,0:T(1,128)}), f32[4,1,8192]{2,1,0:T(1,128)S(1)}, u32[]{:S(2)}, u32[]{:S(2)}) async-start(f32[4,1,8192]{2,1,0:T(1,128)} %reshape.156), calls=%async_computation.1 | async-start | bytes 262144 | tf_op jit(solution)/shard_map/all_to_all | solution.py:234
  33.8 1.6 %copy-done.2 = bf16[128,8192]{1,0:T(8,128)(2,1)S(1)} copy-done((bf16[128,8192]{1,0:T(8,128)(2,1)S(1)}, bf16[128,8192]{1,0:T(8,128)(2,1)}, u32[]{:S(2)}) %copy-start.2) | copy-done | bytes 2097176
  35.4 1.3 %copy-done.7 = f32[256,1280]{1,0:T(8,128)S(1)} copy-done((f32[256,1280]{1,0:T(8,128)S(1)}, f32[256,1280]{1,0:T(8,128)}, u32[]{:S(2)}) %copy-start.7) | copy-done | bytes 1310744
  36.7 8.2 %projection.4.refs_11_ = f32[256,1280]{1,0:T(8,128)S(1)} custom-call(bf16[128,8192]{1,0:T(8,128)(2,1)S(1)} %copy-done.2, bf16[8192,2,1280]{2,1,0:T(2,128)(2,1)} %refs_10_.5, bf16[8192,2,1280]{2,1,0:T(2,128)(2,1)} %refs_10_.5, bf16[8192,2,1280]{2,1,0:T(2,128)(2,1)} %refs_10_.5, bf16[8192,2,1280]{2,1,0:T(2,128)(2,1)} %refs_10_.5, ...), custom_call_target="tpu_custom_call" | custom-call | flops 2684354560 | bytes 10485760 | tf_op jit(solution)/shard_map/projection/pallas_call | solution.py:73
  45.5 5.1 %all-to-all-start.3 = ((bf16[4,2,32,256]{3,2,1,0:T(8,128)(2,1)}), bf16[4,2,32,256]{3,2,1,0:T(8,128)(2,1)S(1)}, u32[]{:S(2)}, u32[]{:S(2)}) async-start(bf16[4,2,32,256]{3,2,1,0:T(8,128)(2,1)} %bitcast.64), calls=%async_computation.3 | async-start | bytes 262144 | tf_op jit(solution)/shard_map/all_to_all | solution.py:226
  51.2 2.6 %reduce = f32[4,8192]{1,0:T(4,128)} reduce(f32[4,1,8192]{2,1,0:T(1,128)} %copy-done.13, f32[]{:T(128)} %broadcast.172), dimensions={1}, to_apply=%all_to_all.13.reduce_sub_computation | reduce | bytes 262148 | tf_op jit(solution)/shard_map/all_to_all | solution.py:234
  53.8 1.8 %reshape.157 = f32[4,8,16,64]{3,2,1,0:T(8,128)} reshape(f32[4,8192]{1,0:T(4,128)} %reduce) | data formatting | bytes 262144
  55.5 1.6 %reduce_sum.49 = bf16[8,16,64]{2,1,0:T(8,128)(2,1)} reduce(f32[4,8,16,64]{3,2,1,0:T(8,128)} %reshape.157, f32[]{:T(128)} %constant.51.clone.1), dimensions={0}, to_apply=%region_4.5 | reduce | flops 24576 | bytes 147460 | tf_op jit(solution)/shard_map/reduce_sum | solution.py:235
  57.1 3.3 %fusion.5 = bf16[8,2,16,1280]{3,2,1,0:T(8,128)(2,1)} fusion(bf16[8,64,2,1280]{3,2,1,0:T(2,128)(2,1)} %param.12, pred[8,16,8]{1,2,0:T(8,128)(4,1)S(1)} %iota_compare_fusion.5, bf16[8,16,64]{2,1,0:T(8,128)(2,1)} %reduce_sum.49), kind=kOutput, calls=%fused_computation.4 | convolution fusion | flops 335937536 | bytes 3294208 | tf_op jit(solution)/shard_map/oxbl,blpj->opxj/dot_general | solution.py:237
  60.4 4.4 %all-to-all-start.2 = ((bf16[8,2,16,1280]{3,2,1,0:T(8,128)(2,1)}), bf16[8,2,16,1280]{3,2,1,0:T(8,128)(2,1)}, u32[]{:S(2)}, u32[]{:S(2)}) async-start(bf16[8,2,16,1280]{3,2,1,0:T(8,128)(2,1)} %fusion.5), calls=%async_computation.2 | async-start | bytes 1310720 | tf_op jit(solution)/shard_map/all_to_all | solution.py:240
  64.8 1.5 %broadcast_subtract_fusion.ids_ref = s32[128,4]{1,0:T(8,128)} fusion(s32[128,4]{1,0:T(8,128)} %copy.23, s32[]{:T(128)S(6)} %mul.49), kind=kLoop, calls=%fused_computation.28 | loop fusion | flops 512 | bytes 4100 | tf_op jit(solution)/shard_map/sub | solution.py:254
  66.3 1.6 %copy-done.3 = bf16[128,8192]{1,0:T(8,128)(2,1)S(1)} copy-done((bf16[128,8192]{1,0:T(8,128)(2,1)S(1)}, bf16[128,8192]{1,0:T(8,128)(2,1)}, u32[]{:S(2)}) %copy-start.3) | copy-done | bytes 2097176
  67.9 11.4 %projection.5.plain_ref = f32[256,1280]{1,0:T(8,128)S(1)} custom-call(bf16[128,8192]{1,0:T(8,128)(2,1)S(1)} %copy-done.3, bf16[8192,2,1280]{2,1,0:T(2,128)(2,1)} %refs_10_.5, bf16[8192,2,1280]{2,1,0:T(2,128)(2,1)} %refs_10_.5, bf16[8192,2,1280]{2,1,0:T(2,128)(2,1)} %refs_10_.5, bf16[8192,2,1280]{2,1,0:T(2,128)(2,1)} %refs_10_.5, ...), custom_call_target="tpu_custom_call" | custom-call | flops 4026531840 | bytes 15728640 | tf_op jit(solution)/shard_map/projection/pallas_call | solution.py:73
  79.3 1.1 %copy-done.4 = f32[256,1280]{1,0:T(8,128)} copy-done((f32[256,1280]{1,0:T(8,128)}, f32[256,1280]{1,0:T(8,128)S(1)}, u32[]{:S(2)}) %copy-start.4) | copy-done | bytes 1310744
  80.3 1.3 %copy-done.5 = f32[256,1280]{1,0:T(8,128)S(1)} copy-done((f32[256,1280]{1,0:T(8,128)S(1)}, f32[256,1280]{1,0:T(8,128)}, u32[]{:S(2)}) %copy-start.5) | copy-done | bytes 1310744
  81.7 0.8 copy-done.8
  82.5 0.8 copy-done.9
  83.3 0.8 copy-done.10
  84.2 0.8 copy-done.11
  85.0 0.8 copy-done.12
  85.9 4.8 %attention.1 = bf16[2,128,1024]{2,1,0:T(8,128)(2,1)S(1)} custom-call(f32[256,1280]{1,0:T(8,128)S(1)} %copy-done.5, bf16[8,2,16,1280]{3,2,1,0:T(8,128)(2,1)} %all-to-all-done.2.back_ref, s32[128,1]{1,0:T(8,128)S(1)} %copy-done.10, s32[128,1]{1,0:T(8,128)S(1)} %copy-done.11, s32[128,4]{1,0:T(8,128)S(1)} %copy-done.12, f32[128,128]{1,0:T(8,128)S(1)} %copy-done.8, ...), custom_call_target="tpu_custom_call" | custom-call | tf_op jit(solution)/shard_map/attention/pallas_call | solution.py:161
  90.6 1.3 %copy.28 = bf16[128,2,1024]{2,1,0:T(2,128)(2,1)} copy(bf16[128,2,1024]{2,0,1:T(8,128)(2,1)S(1)} %bitcast.63) | data formatting | bytes 1048576 | tf_op jit(solution)/shard_map/transpose | solution.py:261
  (42 shorter events, 4.2 us)
Async XLA Ops:
  0.0 26.9 %copy-start = (bf16[8,2048,64]{1,2,0:T(8,128)(2,1)S(1)}, bf16[8,2048,64]{1,2,0:T(8,128)(2,1)}, u32[]{:S(2)}) copy-start(bf16[8,2048,64]{1,2,0:T(8,128)(2,1)} %param.11) | copy-start | bytes 6291460
  0.0 9.6 %copy-start.16 = (s32[128]{0:T(128)S(1)}, s32[128]{0:T(128)}, u32[]{:S(2)}) copy-start(s32[128]{0:T(128)} %param.16) | copy-start | bytes 1540
  0.0 10.3 %copy-start.15 = (s32[128,4]{0,1:T(4,128)S(1)}, s32[128,4]{0,1:T(4,128)}, u32[]{:S(2)}) copy-start(s32[128,4]{0,1:T(4,128)} %param.15) | copy-start | bytes 6148
  0.0 11.1 %copy-start.14 = (bf16[32,8,256]{2,1,0:T(8,128)(2,1)S(1)}, bf16[32,8,256]{2,1,0:T(8,128)(2,1)}, u32[]{:S(2)}) copy-start(bf16[32,8,256]{2,1,0:T(8,128)(2,1)} %param.17) | copy-start | bytes 393220
  3.4 23.5 %all-to-all-start = ((bf16[8,16,2048]{2,1,0:T(8,128)(2,1)}), bf16[8,16,2048]{2,1,0:T(8,128)(2,1)S(1)}, u32[]{:S(2)}, u32[]{:S(2)}) async-start(bf16[8,16,2048]{2,1,0:T(8,128)(2,1)} %bitcast.2), calls=%async_computation | async-start | bytes 1048576 | tf_op jit(solution)/shard_map/all_to_all | solution.py:220
  12.8 1.6 %copy-start.1 = (bf16[128,8192]{1,0:T(8,128)(2,1)S(1)}, bf16[128,8192]{1,0:T(8,128)(2,1)}, u32[]{:S(2)}) copy-start(bf16[128,8192]{1,0:T(8,128)(2,1)} %refs_0_.5) | copy-start | bytes 6291460
  25.8 1.1 %copy-start.6 = (f32[256,1280]{1,0:T(8,128)}, f32[256,1280]{1,0:T(8,128)S(1)}, u32[]{:S(2)}) copy-start(f32[256,1280]{1,0:T(8,128)S(1)} %projection.3.refs_11_) | copy-start | bytes 3932164
  28.9 15.9 %all-to-all-start.1 = ((f32[4,1,8192]{2,1,0:T(1,128)}), f32[4,1,8192]{2,1,0:T(1,128)S(1)}, u32[]{:S(2)}, u32[]{:S(2)}) async-start(f32[4,1,8192]{2,1,0:T(1,128)} %reshape.156), calls=%async_computation.1 | async-start | bytes 262144 | tf_op jit(solution)/shard_map/all_to_all | solution.py:234
  33.8 1.6 %copy-start.2 = (bf16[128,8192]{1,0:T(8,128)(2,1)S(1)}, bf16[128,8192]{1,0:T(8,128)(2,1)}, u32[]{:S(2)}) copy-start(bf16[128,8192]{1,0:T(8,128)(2,1)} %refs_0_.5) | copy-start | bytes 6291460
  35.4 1.3 %copy-start.7 = (f32[256,1280]{1,0:T(8,128)S(1)}, f32[256,1280]{1,0:T(8,128)}, u32[]{:S(2)}) copy-start(f32[256,1280]{1,0:T(8,128)} %copy-done.6) | copy-start | bytes 3932164
  44.9 0.7 copy-start.13
  45.5 14.9 %all-to-all-start.3 = ((bf16[4,2,32,256]{3,2,1,0:T(8,128)(2,1)}), bf16[4,2,32,256]{3,2,1,0:T(8,128)(2,1)S(1)}, u32[]{:S(2)}, u32[]{:S(2)}) async-start(bf16[4,2,32,256]{3,2,1,0:T(8,128)(2,1)} %bitcast.64), calls=%async_computation.3 | async-start | bytes 262144 | tf_op jit(solution)/shard_map/all_to_all | solution.py:226
  60.4 19.9 %all-to-all-start.2 = ((bf16[8,2,16,1280]{3,2,1,0:T(8,128)(2,1)}), bf16[8,2,16,1280]{3,2,1,0:T(8,128)(2,1)}, u32[]{:S(2)}, u32[]{:S(2)}) async-start(bf16[8,2,16,1280]{3,2,1,0:T(8,128)(2,1)} %fusion.5), calls=%async_computation.2 | async-start | bytes 1310720 | tf_op jit(solution)/shard_map/all_to_all | solution.py:240
  66.3 1.6 %copy-start.3 = (bf16[128,8192]{1,0:T(8,128)(2,1)S(1)}, bf16[128,8192]{1,0:T(8,128)(2,1)}, u32[]{:S(2)}) copy-start(bf16[128,8192]{1,0:T(8,128)(2,1)} %refs_0_.5) | copy-start | bytes 6291460
  79.2 1.1 %copy-start.4 = (f32[256,1280]{1,0:T(8,128)}, f32[256,1280]{1,0:T(8,128)S(1)}, u32[]{:S(2)}) copy-start(f32[256,1280]{1,0:T(8,128)S(1)} %projection.5.plain_ref) | copy-start | bytes 3932164
  80.3 1.3 %copy-start.5 = (f32[256,1280]{1,0:T(8,128)S(1)}, f32[256,1280]{1,0:T(8,128)}, u32[]{:S(2)}) copy-start(f32[256,1280]{1,0:T(8,128)} %copy-done.4) | copy-start | bytes 3932164
  81.7 0.8 copy-start.8
  82.5 0.8 copy-start.9
  83.3 0.8 copy-start.10
  84.2 0.8 copy-start.11
  85.0 0.8 copy-start.12

commit v2 on v1

--- a/solution.py
+++ b/solution.py
@@ -168,6 +168,331 @@
     )(plain, back, dest, lens, ids, cosine, sine, pool)
 
 
+MESH = pl.DeviceIdType.MESH
+DOWN_STEP = 5
+UP_STEP = 9
+
+
+def attend_rows(plain_ref, back_ref, pick, live, cosine, sine, pool_ref, out_ref):
+    heads, rows, _ = out_ref.shape
+    slots = back_ref.shape[0] * back_ref.shape[2]
+    count = pool_ref.shape[0] * pool_ref.shape[2]
+    scale = 1.0 / HEAD_SIZE**0.5
+
+    def rope(v):
+        return (v * cosine + pltpu.roll(v, HEAD_SIZE // 2, 1) * sine).astype(jnp.bfloat16)
+
+    for h in range(heads):
+        update = jnp.dot(
+            pick, back_ref[:, h].reshape(slots, back_ref.shape[3]), preferred_element_type=jnp.float32
+        )
+        joined = plain_ref[h * rows : (h + 1) * rows, :] + ADAPTER_SCALE * update
+        key_new = rope(joined[:, QUERY_PER_KEY * HEAD_SIZE : (QUERY_PER_KEY + 1) * HEAD_SIZE])
+        key_new = key_new.astype(jnp.float32)
+        value_new = joined[:, (QUERY_PER_KEY + 1) * HEAD_SIZE :].astype(jnp.bfloat16)
+        value_new = value_new.astype(jnp.float32)
+        keys = pool_ref[:, h, :, :HEAD_SIZE].reshape(count, HEAD_SIZE)
+        value_rows = pool_ref[:, h, :, HEAD_SIZE:].reshape(count, HEAD_SIZE)
+        for g in range(QUERY_PER_KEY):
+            query = rope(joined[:, g * HEAD_SIZE : (g + 1) * HEAD_SIZE])
+            scores = (
+                lax.dot_general(
+                    query, keys, (((1,), (1,)), ((), ())), preferred_element_type=jnp.float32
+                )
+                * scale
+            )
+            own = jnp.sum(query.astype(jnp.float32) * key_new, axis=1, keepdims=True) * scale
+            scores = jnp.where(live > 0.0, scores, -jnp.inf)
+            top = jnp.maximum(jnp.max(scores, axis=1, keepdims=True), own)
+            prob = jnp.exp(scores - top)
+            prob_own = jnp.exp(own - top)
+            total = jnp.sum(prob, axis=1, keepdims=True) + prob_own
+            mixed = jnp.dot(prob.astype(jnp.bfloat16), value_rows, preferred_element_type=jnp.float32)
+            mixed = mixed + prob_own.astype(jnp.bfloat16).astype(jnp.float32) * value_new
+            out_ref[h, :, g * HEAD_SIZE : (g + 1) * HEAD_SIZE] = (mixed / total).astype(jnp.bfloat16)
+
+
+def step_kernel(n_store, n_ctx, shard_adapters, tiles, *refs):
+    tok_ref = refs[0]
+    w_refs = refs[1 : 1 + tiles]
+    (tok_hbm, down_hbm, up_hbm, pool_hbm, adapter_ref, slot_ref, ids_ref, len_ref, freq_ref, out_ref) = refs[
+        1 + tiles : 11 + tiles
+    ]
+    (e_ref, z_ref, plain, xl, down, up, out_s, recv_s, part, sb, bk, poolr, place_s, hot_s, live_s,
+     cos_s, sin_s, in_sem, up_sem, s1, r1, s2, r2, s3, r3, s4, r4) = refs[11 + tiles :]
+    step = pl.program_id(0)
+    last = pl.num_programs(0) - 1
+    me = lax.axis_index("store")
+    member = lax.axis_index("ctx")
+    rows = tok_ref.shape[0]
+    depth = tok_ref.shape[1]
+    slots = n_store * CAP
+    wide = down.shape[0]
+    width = xl.shape[1]
+
+    def store_copy(src, dst, send, recv, d):
+        target = lax.rem(me + d, n_store)
+        source = lax.rem(me + n_store - d, n_store)
+        go = pltpu.make_async_remote_copy(
+            src_ref=src.at[target], dst_ref=dst.at[me], send_sem=send.at[d - 1],
+            recv_sem=recv.at[d - 1], device_id={"store": target}, device_id_type=MESH)
+        come = pltpu.make_async_remote_copy(
+            src_ref=src.at[target], dst_ref=dst.at[source], send_sem=send.at[d - 1],
+            recv_sem=recv.at[d - 1], device_id={"store": target}, device_id_type=MESH)
+        return go, come
+
+    def ctx_copy(src, dst, send, recv, d, by_target):
+        target = lax.rem(member + d, n_ctx)
+        source = lax.rem(member + n_ctx - d, n_ctx)
+        origin = src.at[target] if by_target else src.at[member]
+        go = pltpu.make_async_remote_copy(
+            src_ref=origin, dst_ref=dst.at[member], send_sem=send.at[d - 1],
+            recv_sem=recv.at[d - 1], device_id={"ctx": target}, device_id_type=MESH)
+        come = pltpu.make_async_remote_copy(
+            src_ref=origin, dst_ref=dst.at[source], send_sem=send.at[d - 1],
+            recv_sem=recv.at[d - 1], device_id={"ctx": target}, device_id_type=MESH)
+        return go, come
+
+    def local_copies():
+        start = pl.multiple_of(member * width, width)
+        first = pltpu.make_async_copy(tok_hbm.at[:, pl.ds(start, width)], xl, in_sem.at[0])
+        second = pltpu.make_async_copy(down_hbm, down, in_sem.at[1])
+        third = pltpu.make_async_copy(pool_hbm.at[member], poolr.at[member], in_sem.at[2])
+        rest = [
+            pltpu.make_async_copy(up_hbm.at[:, :, pl.ds(c * LANES, LANES)], up.at[c], up_sem.at[c])
+            for c in range(tiles)
+        ]
+        return first, second, third, rest
+
+    @pl.when(step == 0)
+    def _():
+        barrier = pltpu.get_barrier_semaphore()
+        for d in range(1, n_store):
+            pl.semaphore_signal(barrier, inc=1, device_id={"store": lax.rem(me + d, n_store)}, device_id_type=MESH)
+        for d in range(1, n_ctx):
+            pl.semaphore_signal(barrier, inc=1, device_id={"ctx": lax.rem(member + d, n_ctx)}, device_id_type=MESH)
+        first, second, third, rest = local_copies()
+        first.start()
+        second.start()
+        third.start()
+        for copy in rest:
+            copy.start()
+        row = lax.broadcasted_iota(jnp.int32, (LANES, 4 * LANES), 0)
+        col = lax.broadcasted_iota(jnp.int32, (LANES, 4 * LANES), 1)
+        goal = jnp.where(col < 2 * LANES, 2 * row, 2 * row + 1 + 2 * LANES)
+        e_ref[...] = (col == goal).astype(jnp.float32).astype(jnp.bfloat16)
+        plain[...] = jnp.zeros_like(plain)
+
+        adapters = adapter_ref[...]
+        chosen = jnp.zeros_like(adapters)
+        for a in range(slot_ref.shape[0]):
+            chosen = jnp.where(adapters == a, slot_ref[a], chosen)
+        owner = chosen // shard_adapters
+        local = (chosen - owner * shard_adapters).astype(jnp.float32)
+        before = lax.broadcasted_iota(jnp.int32, (rows, rows), 0)
+        after = lax.broadcasted_iota(jnp.int32, (rows, rows), 1)
+        earlier = (before < after).astype(jnp.float32).astype(jnp.bfloat16)
+        rank = jnp.zeros(owner.shape, jnp.float32)
+        for w in range(n_store):
+            mine = (owner == w).astype(jnp.float32)
+            counted = jnp.dot(mine.astype(jnp.bfloat16), earlier, preferred_element_type=jnp.float32)
+            rank = rank + mine * counted
+        dest = owner.astype(jnp.float32) * CAP + rank
+        which = lax.broadcasted_iota(jnp.int32, owner.shape, 0)
+        dest_mine = jnp.sum(jnp.where(which == me, dest, 0.0), axis=0, keepdims=True)
+        slot_id = lax.broadcasted_iota(jnp.int32, (slots, rows), 0).astype(jnp.float32)
+        place = (slot_id == dest_mine).astype(jnp.float32)
+        place_s[...] = place
+        here = jnp.where(owner == me, rank, -1.0)
+        cap_id = lax.broadcasted_iota(jnp.int32, (CAP, rows), 0).astype(jnp.float32)
+        arrived = jnp.concatenate(
+            [
+                jnp.sum(jnp.where(cap_id == here[o : o + 1, :], local[o : o + 1, :] + 1.0, 0.0), axis=1, keepdims=True)
+                for o in range(n_store)
+            ],
+            axis=0,
+        )
+        adapter_id = (lax.broadcasted_iota(jnp.int32, (slots, wide), 1) // (wide // shard_adapters)).astype(jnp.float32)
+        hot_s[...] = (adapter_id + 1.0 == arrived).astype(jnp.float32)
+
+        first.wait()
+        out_s[...] = jnp.dot(
+            place.astype(jnp.bfloat16), xl[...], preferred_element_type=jnp.float32
+        ).astype(jnp.bfloat16).reshape(n_store, CAP, width)
+        recv_s[pl.ds(me, 1)] = out_s[pl.ds(me, 1)]
+        pl.semaphore_wait(barrier, n_store + n_ctx - 2)
+        for d in range(1, n_store):
+            store_copy(out_s, recv_s, s1, r1, d)[0].start()
+        for d in range(1, n_ctx):
+            ctx_copy(pool_hbm, poolr, s4, r4, d, True)[0].start()
+
+    @pl.when(step == 1)
+    def _():
+        count = live_s.shape[1]
+        token = lax.broadcasted_iota(jnp.int32, (count, rows), 0)
+        block, offset = token // BLK, token % BLK
+        live = jnp.zeros((count, rows), jnp.float32)
+        for j in range(ids_ref.shape[0]):
+            hit = (ids_ref[j : j + 1, :] - me * (count // BLK) == block) & (offset + j * BLK < len_ref[...])
+            live = jnp.where(hit, 1.0, live)
+        live_s[...] = live.T
+        lens = jnp.broadcast_to(len_ref[...].astype(jnp.float32), (rows, rows)).T
+        angle = lens * freq_ref[...]
+        cos_s[...] = jnp.cos(angle)
+        lane = lax.broadcasted_iota(jnp.int32, (rows, HEAD_SIZE), 1)
+        sine = jnp.sin(angle)
+        sin_s[...] = jnp.where(lane < HEAD_SIZE // 2, -sine, sine)
+
+    @pl.when(step == DOWN_STEP)
+    def _():
+        for d in range(1, n_store):
+            go, come = store_copy(out_s, recv_s, s1, r1, d)
+            go.wait_send()
+            come.wait_recv()
+        local_copies()[1].wait()
+        value = lax.dot_general(
+            recv_s[...].reshape(slots, width), down[...], (((1,), (1,)), ((), ())),
+            preferred_element_type=jnp.float32)
+        value = jnp.where(hot_s[...] > 0.0, value, 0.0)
+        folded = value[:, :LANES]
+        for c in range(1, wide // LANES):
+            folded = folded + value[:, c * LANES : (c + 1) * LANES]
+        part[member] = folded
+        for d in range(1, n_ctx):
+            ctx_copy(part, part, s2, r2, d, False)[0].start()
+
+    @pl.when(step == UP_STEP)
+    def _():
+        for d in range(1, n_ctx):
+            go, come = ctx_copy(part, part, s2, r2, d, False)
+            go.wait_send()
+            come.wait_recv()
+        for copy in local_copies()[3]:
+            copy.wait()
+        total = part[0]
+        for c in range(1, n_ctx):
+            total = total + part[c]
+        total = (total + pltpu.roll(total, LANES // 2, 1)).astype(jnp.bfloat16).astype(jnp.float32)
+        for c in range(wide // LANES):
+            cols = slice(c * LANES, (c + 1) * LANES)
+            spread = (total * hot_s[:, cols]).astype(jnp.bfloat16)
+            pair = jnp.dot(spread, e_ref[...], preferred_element_type=jnp.float32).astype(jnp.bfloat16)
+            z_ref[:slots, 2 * c * LANES : 2 * (c + 1) * LANES] = pair[:, : 2 * LANES]
+            z_ref[slots:, 2 * c * LANES : 2 * (c + 1) * LANES] = pair[:, 2 * LANES :]
+        for j in range(0, tiles, 2):
+            weight = jnp.concatenate(
+                [up.at[i].reshape(2 * wide, LANES)[...] for i in (j, j + 1)], axis=1)
+            update = jnp.dot(z_ref[:, : 2 * wide], weight, preferred_element_type=jnp.float32).astype(jnp.bfloat16)
+            cols = slice(j * LANES, (j + 2) * LANES)
+            for h in range(2):
+                sb[:, h, :, cols] = update[h * slots : (h + 1) * slots].reshape(n_store, CAP, 2 * LANES)
+        bk[pl.ds(me, 1)] = sb[pl.ds(me, 1)]
+        for d in range(1, n_store):
+            store_copy(sb, bk, s3, r3, d)[0].start()
+
+    spread_columns(tok_ref, e_ref, z_ref)
+    for j in range(0, tiles, 2):
+        weight = jnp.concatenate(
+            [w_refs[i].reshape(2 * depth, LANES)[...] for i in (j, j + 1)], axis=1)
+        cols = slice(j * LANES, (j + 2) * LANES)
+        plain[:, cols] += jnp.dot(z_ref[...], weight, preferred_element_type=jnp.float32)
+
+    @pl.when(step == last)
+    def _():
+        local_copies()[2].wait()
+        for d in range(1, n_ctx):
+            go, come = ctx_copy(pool_hbm, poolr, s4, r4, d, True)
+            go.wait_send()
+            come.wait_recv()
+        for d in range(1, n_store):
+            go, come = store_copy(sb, bk, s3, r3, d)
+            go.wait_send()
+            come.wait_recv()
+        pick = place_s[...].T.astype(jnp.bfloat16)
+        attend_rows(plain, bk, pick, live_s[...], cos_s[...], sin_s[...], poolr, out_ref)
+
+
+def fused(tokens, joined_weight, down_weight, up_weight, adapter_per_request, adapter_store_slot,
+          prefix_block_list, prefix_length, key_value_pool):
+    n_store = lax.axis_size("store")
+    n_ctx = lax.axis_size("ctx")
+    rows, d_model = tokens.shape
+    shard_adapters, width, rank_size = down_weight.shape
+    heads, columns = joined_weight.shape[1:]
+    tiles = columns // LANES
+    pool_rows = key_value_pool.shape[0]
+    slots = n_store * CAP
+    wide = shard_adapters * rank_size
+    bf, f32 = jnp.bfloat16, jnp.float32
+    down = jnp.transpose(down_weight, (0, 2, 1)).reshape(wide, width)
+    up = up_weight.reshape(wide, heads, columns)
+    pool = jnp.transpose(key_value_pool, (1, 0, 2)).reshape(n_ctx, heads, pool_rows, 2 * HEAD_SIZE)
+    half = HEAD_SIZE // 2
+    freq = jnp.power(ROPE_THETA, -(jnp.arange(half, dtype=f32) * 2.0 / HEAD_SIZE))
+    freq = jnp.concatenate([freq, freq])[None]
+    hbm = pl.BlockSpec(memory_space=pl.ANY)
+
+    def whole_block(shape):
+        return pl.BlockSpec(shape, lambda k: (0, 0))
+
+    in_specs = [pl.BlockSpec((rows, DEPTH), lambda k: (0, k))]
+    for c in range(tiles):
+        in_specs.append(pl.BlockSpec((DEPTH, 2, LANES), functools.partial(lambda c, k: (k, 0, c), c)))
+    in_specs += [hbm] * 4 + [
+        whole_block((n_store, rows)),
+        pl.BlockSpec(memory_space=pltpu.SMEM),
+        whole_block(prefix_block_list.shape[::-1]),
+        whole_block((1, rows)),
+        whole_block((1, HEAD_SIZE)),
+    ]
+    dma = pltpu.SemaphoreType.DMA
+    out = pl.pallas_call(
+        functools.partial(step_kernel, n_store, n_ctx, shard_adapters, tiles),
+        grid=(d_model // DEPTH,),
+        in_specs=in_specs,
+        out_specs=pl.BlockSpec((heads, rows, QUERY_PER_KEY * HEAD_SIZE), lambda k: (0, 0, 0)),
+        out_shape=jax.ShapeDtypeStruct((heads, rows, QUERY_PER_KEY * HEAD_SIZE), bf),
+        scratch_shapes=[
+            pltpu.VMEM((LANES, 4 * LANES), bf),
+            pltpu.VMEM((2 * rows, 2 * DEPTH), bf),
+            pltpu.VMEM((2 * rows, columns), f32),
+            pltpu.VMEM((rows, width), bf),
+            pltpu.VMEM((wide, width), bf),
+            pltpu.VMEM((tiles, wide, 2, LANES), bf),
+            pltpu.VMEM((n_store, CAP, width), bf),
+            pltpu.VMEM((n_store, CAP, width), bf),
+            pltpu.VMEM((n_ctx, slots, LANES), f32),
+            pltpu.VMEM((n_store, heads, CAP, columns), bf),
+            pltpu.VMEM((n_store, heads, CAP, columns), bf),
+            pltpu.VMEM((n_ctx, heads, pool_rows, 2 * HEAD_SIZE), bf),
+            pltpu.VMEM((slots, rows), f32),
+            pltpu.VMEM((slots, wide), f32),
+            pltpu.VMEM((rows, n_ctx * pool_rows), f32),
+            pltpu.VMEM((rows, HEAD_SIZE), f32),
+            pltpu.VMEM((rows, HEAD_SIZE), f32),
+            dma((3,)),
+            dma((tiles,)),
+            dma((n_store - 1,)),
+            dma((n_store - 1,)),
+            dma((n_ctx - 1,)),
+            dma((n_ctx - 1,)),
+            dma((n_store - 1,)),
+            dma((n_store - 1,)),
+            dma((n_ctx - 1,)),
+            dma((n_ctx - 1,)),
+        ],
+        compiler_params=pltpu.CompilerParams(
+            vmem_limit_bytes=48 << 20, collective_id=0, has_side_effects=True
+        ),
+        name="decode_step",
+    )(
+        tokens, *([joined_weight] * tiles), tokens, down, up, pool,
+        adapter_per_request.reshape(n_store, rows), adapter_store_slot, prefix_block_list.T,
+        prefix_length[None], freq,
+    )
+    return jnp.transpose(out, (1, 0, 2))
+
+
 def routing(adapter_per_request, adapter_store_slot, shards, request_shard, shard_adapters, shard):
     adapters = adapter_store_slot.shape[0]
     match = adapter_per_request[:, None] == jnp.arange(adapters, dtype=jnp.int32)[None, :]
@@ -208,6 +533,20 @@
     shard_adapters, width_slice, rank_size = down_weight.shape
     head_slice = joined_weight.shape[1]
     columns = joined_weight.shape[2]
+    slots = n_store * CAP
+    if (
+        head_slice == 2
+        and slots == request_shard
+        and tokens.shape[1] % DEPTH == 0
+        and tokens.shape[1] // DEPTH > UP_STEP + 1
+        and shard_adapters * rank_size <= DEPTH
+        and rank_size * 2 == LANES
+        and columns % (2 * LANES) == 0
+    ):
+        return fused(
+            tokens, joined_weight, down_weight, up_weight, adapter_per_request, adapter_store_slot,
+            prefix_block_list, prefix_length, key_value_pool,
+        )
     pool_rows = key_value_pool.shape[0]
 
     dest, arrived = routing(

time: 93.4 us -> 50.3 us (0.54); the launches traced: 92 us -> 50 us
  starting transfers between devices: 19.5 us -> 0 us
  local copies, waits for them, and re-layouts: 21.9 us -> 8.12 us
  other arithmetic: 8.15 us -> 0.09 us
  matrix products: 6.63 us -> 0 us
  Pallas kernels: 35.6 us -> 41.8 us
    all_to_all x4 -> x0, starting transfers between devices: 19.5 us -> none  [the longest x1 5.18 us: body(): lax.all_to_all(outgoing.reshape(n_store, CAP, width_slice), 'store', spli...]
    unnamed x37 -> x12, local copies, waits for them, and re-layouts: 17.8 us -> 5.85 us
    dot_general x3 -> x0, matrix products: 6.63 us -> none  [the longest x1 3.28 us: body(): jnp.einsum('oxbl,blpj->opxj', spread_rows, up_weight, preferred_element_t...]
    pallas_call x4 -> x1, Pallas kernels: 35.6 us -> 41.8 us  [fused(): pl.pallas_call(functools.partial(step_kernel, n_store, n_ctx, shard_adapt...]
    reduce_sum x4 -> x0, other arithmetic: 2.96 us -> none  [the longest x1 1.58 us: body(): shrunk = jnp.sum(partials, axis=0).astype(jnp.bfloat16)]
    all_to_all x1 -> x0, other arithmetic: 2.57 us -> none  [body(): lax.all_to_all(copies, 'ctx', split_axis=0, concat_axis=0, tiled=True)]
    sub x2 -> x0, other arithmetic: 1.48 us -> none  [the longest x1 1.48 us: body(): prefix_block_list - shard * group_blocks]
  transfers between devices with their start and end apart: 4 -> 0, of which waited for: 0 -> 0; matrix products, arithmetic and copies ran while one was open for 17% -> 0% of each run, Pallas kernels for 34% -> 0%
where the time goes in v2:
time: 50.3 us; the launch traced here: 50 us
  Pallas kernels  41.8 us (83%)
  local copies, waits for them, and re-layouts  8.12 us (16%)
    pallas_call x1, Pallas kernels, fused(): pl.pallas_call(functools.partial(step_kernel, n_store, n_ctx, shard_adapt...  41.8 us
    unnamed x12, local copies, waits for them, and re-layouts  5.85 us
    transpose x1, local copies, waits for them, and re-layouts, fused(): return jnp.transpose(out, (1, 0, 2))  1.33 us

profile of v2, /device:TPU:0, one launch (start us, length us, event | category | flops | bytes accessed | tf_op | source)
XLA Modules:
  0.0 50.0 jit_solution(3846110048480878948)
XLA Ops:
  0.0 0.1 maximum_bitcast_fusion.refs_19_
  0.1 0.9 %copy.10 = bf16[8,32,256]{2,1,0:T(8,128)(2,1)S(1)} copy(bf16[8,32,256]{2,0,1:T(8,128)(2,1)} %bitcast.19) | data formatting | bytes 262144 | tf_op jit(solution)/shard_map/transpose | solution.py:429
  1.0 0.0 copy-start
  1.0 1.6 %copy-done = bf16[128,8192]{1,0:T(8,128)(2,1)S(1)} copy-done((bf16[128,8192]{1,0:T(8,128)(2,1)S(1)}, bf16[128,8192]{1,0:T(8,128)(2,1)}, u32[]{:S(2)}) %copy-start) | copy-done | bytes 2097176
  2.6 0.0 copy-start.1
  2.6 1.6 %copy-done.1 = bf16[8,2048,64]{1,2,0:T(8,128)(2,1)S(1)} copy-done((bf16[8,2048,64]{1,2,0:T(8,128)(2,1)S(1)}, bf16[8,2048,64]{1,2,0:T(8,128)(2,1)}, u32[]{:S(2)}) %copy-start.1) | copy-done | bytes 2097176
  4.2 0.0 copy-start.2
  4.2 0.7 %copy-done.2 = s32[1024]{0:T(1024)S(1)} copy-done((s32[1024]{0:T(1024)S(1)}, s32[1024]{0:T(1024)}, u32[]{:S(2)}) %copy-start.2) | copy-done | bytes 4120
  4.9 0.0 copy-start.3
  4.9 0.7 %copy-done.3 = s32[128,4]{0,1:T(4,128)S(1)} copy-done((s32[128,4]{0,1:T(4,128)S(1)}, s32[128,4]{0,1:T(4,128)}, u32[]{:S(2)}) %copy-start.3) | copy-done | bytes 2072
  5.6 0.0 copy-start.4
  5.6 0.7 %copy-done.4 = s32[64]{0:T(128)S(1)} copy-done((s32[64]{0:T(128)S(1)}, s32[64]{0:T(128)}, u32[]{:S(2)}) %copy-start.4) | copy-done | bytes 280
  6.2 0.0 copy-start.5
  6.2 0.7 %copy-done.5 = s32[128]{0:T(128)S(1)} copy-done((s32[128]{0:T(128)S(1)}, s32[128]{0:T(128)}, u32[]{:S(2)}) %copy-start.5) | copy-done | bytes 536
  6.9 41.8 %decode_step.1 = bf16[2,128,1024]{2,1,0:T(8,128)(2,1)S(1)} custom-call(bf16[128,8192]{1,0:T(8,128)(2,1)S(1)} %copy-done, bf16[8192,2,1280]{2,1,0:T(2,128)(2,1)} %refs_10_.1, bf16[8192,2,1280]{2,1,0:T(2,128)(2,1)} %refs_10_.1, bf16[8192,2,1280]{2,1,0:T(2,128)(2,1)} %refs_10_.1, bf16[8192,2,1280]{2,1,0:T(2,128)(2,1)} %refs_10_.1, ...), custom_call_target="tpu_custom_call" | custom-call | tf_op jit(solution)/shard_map/decode_step/pallas_call | solution.py:449
  48.7 1.3 %copy.11 = bf16[128,2,1024]{2,1,0:T(2,128)(2,1)} copy(bf16[128,2,1024]{2,0,1:T(8,128)(2,1)S(1)} %bitcast.13) | data formatting | bytes 1048576 | tf_op jit(solution)/shard_map/transpose | solution.py:493
  (1 shorter events, 0.0 us)
Async XLA Ops:
  1.0 1.6 %copy-start = (bf16[128,8192]{1,0:T(8,128)(2,1)S(1)}, bf16[128,8192]{1,0:T(8,128)(2,1)}, u32[]{:S(2)}) copy-start(bf16[128,8192]{1,0:T(8,128)(2,1)} %refs_11_.1) | copy-start | bytes 6291460
  2.6 1.6 %copy-start.1 = (bf16[8,2048,64]{1,2,0:T(8,128)(2,1)S(1)}, bf16[8,2048,64]{1,2,0:T(8,128)(2,1)}, u32[]{:S(2)}) copy-start(bf16[8,2048,64]{1,2,0:T(8,128)(2,1)} %param.11) | copy-start | bytes 6291460
  4.2 0.7 %copy-start.2 = (s32[1024]{0:T(1024)S(1)}, s32[1024]{0:T(1024)}, u32[]{:S(2)}) copy-start(s32[1024]{0:T(1024)} %param.13) | copy-start | bytes 12292
  4.9 0.7 %copy-start.3 = (s32[128,4]{0,1:T(4,128)S(1)}, s32[128,4]{0,1:T(4,128)}, u32[]{:S(2)}) copy-start(s32[128,4]{0,1:T(4,128)} %param.15) | copy-start | bytes 6148
  5.6 0.7 %copy-start.4 = (s32[64]{0:T(128)S(1)}, s32[64]{0:T(128)}, u32[]{:S(2)}) copy-start(s32[64]{0:T(128)} %refs_16_.1) | copy-start | bytes 772
  6.2 0.7 %copy-start.5 = (s32[128]{0:T(128)S(1)}, s32[128]{0:T(128)}, u32[]{:S(2)}) copy-start(s32[128]{0:T(128)} %param.16) | copy-start | bytes 1540
